TPU v7x, 256 devices: a whole 4x4x8 slice. The times are simulated.
256 devices in a mesh: group: 16 (over y, x), ingroup: 16 (over z, core).
Axes of the slice: x: 4, y: 4, z: 8, core: 2. Of those that a mesh axis runs over, the one named last changes fastest.
Arguments:
- activations: bfloat16 [16384, 3584], P(('group', 'ingroup')), may hold values from -6 to 6
- gate_weights: bfloat16 [256, 1792, 1024], P(('group', 'ingroup')), may hold values from -0.09375 to 0.09375
- up_weights: bfloat16 [256, 1792, 1024], P(('group', 'ingroup')), may hold values from -0.09375 to 0.09375
- down_weights: bfloat16 [256, 1024, 1792], P(('group', 'ingroup')), may hold values from -0.375 to 0.375
- expert_ids: int32 [16384, 8], P(('group', 'ingroup')), may hold values from 0 to 127, as said below
- gate_scores: int32 [16384, 8], P(('group', 'ingroup')), may hold values from 1 to 15
- arrival_pos: int32 [16384], P(('group', 'ingroup')), may hold values from 0 to 63, as said below
Outputs:
- expert_mix: bfloat16 [16384, 3584], P(('group', 'ingroup'))
Inputs may be any that keep to these rules, and one draw needn't show every extreme that they name: `expert_ids`: each row names 8 different experts, two from each of 4 different groups. Among one device's 64 rows no expert is named more than 6 times and no group by more than 24 rows; on every device some expert is named exactly 6 times and some group by exactly 24 rows. `arrival_pos`: within each device's 64 rows the values are a permutation.
All inputs are finite; a program needn't handle non-finite values.
Results may differ from a plain program's by a relative error of at most 0.0077.
Values may be sent and summed in bfloat16 or wider, within the bound.
No kernel may reach another device: no remote copies, remote signals or barrier semaphores. Data moves between devices by JAX's collectives and lax.ppermute only.
A program may use at most 128 MiB of HBM per device.

v0:
```python
import jax
import jax.numpy as jnp
from jax import lax
from jax.sharding import PartitionSpec as P

TOPG = 4


def from_partner(shard, axis, apart):
    return lax.ppermute(shard, axis, [(i, i ^ 1 << apart) for i in range(lax.axis_size(axis))])


def group_layout(int_table, groups, members, expert_most):
    shaped = int_table.reshape(groups, members // 2, 1, expert_most)
    shaped = jnp.broadcast_to(shaped, (groups, members // 2, 2, expert_most))
    return shaped.reshape(groups, members, expert_most)


def per_device(
    activations, gate_weights, up_weights, down_weights, expert_ids, gate_scores, arrival_pos
):
    groups = lax.axis_size("group")
    members = lax.axis_size("ingroup")
    per_group = members // 2
    experts = groups * per_group
    tok_count = activations.shape[0]
    model_width = activations.shape[1]
    half_width = model_width // 2
    top_picks = expert_ids.shape[1]
    capacity = 2 * top_picks * tok_count
    group_most = min(tok_count, 3 * tok_count * TOPG // (2 * groups))
    expert_most = (2 * group_most + per_group - 1) // per_group
    expert_range = jnp.arange(experts, dtype=jnp.int32)
    pick_hits = (expert_ids[:, :, None] == expert_range[None, None, :]).astype(jnp.int32)
    hit_table = jnp.sum(pick_hits, axis=1)
    occurrence = jnp.cumsum(hit_table, axis=0) - hit_table
    position_range = jnp.arange(tok_count, dtype=jnp.int32)
    arrival_table = (arrival_pos[:, None] == position_range[None, :]).astype(jnp.int32)
    own_counts = jnp.dot(hit_table.T, arrival_table)
    shifts = jnp.arange(32, dtype=jnp.int32)
    flat_bits = own_counts.reshape(-1, 32)
    packed = jnp.sum(jnp.left_shift(flat_bits, shifts[None, :]), axis=1)[None, :]
    my_index = lax.axis_index(("group", "ingroup"))
    piece = lax.all_gather(packed, ("group", "ingroup"), axis=0, tiled=True)
    bit_table = jnp.bitwise_and(jnp.right_shift(piece[:, :, None], shifts[None, None, :]), 1)
    bit_table = bit_table.reshape(piece.shape[0], experts, tok_count)
    source_index = jnp.arange(piece.shape[0], dtype=jnp.int32)
    earlier_flag = (source_index < my_index).astype(jnp.int32)
    prior_part = jnp.sum(bit_table * earlier_flag[:, None, None], axis=0)
    total_part = jnp.sum(bit_table, axis=0)
    earlier = jnp.cumsum(total_part, axis=1) - total_part
    rank_table = earlier + prior_part
    rank_by_token = jnp.dot(arrival_table, rank_table.T)
    pick_rank = jnp.sum(pick_hits * rank_by_token[:, None, :], axis=2)
    pick_occurrence = jnp.sum(pick_hits * occurrence[:, None, :], axis=2)
    kept_mask = (pick_rank < capacity).astype(jnp.int32)
    kept_scores = gate_scores * kept_mask
    weight_sum = jnp.maximum(jnp.sum(kept_scores, axis=1), 1)
    routing = kept_scores.astype(jnp.float32) / weight_sum.astype(jnp.float32)[:, None]
    slot_range = jnp.arange(expert_most, dtype=jnp.int32)
    slot_match = hit_table[:, :, None] * (
        occurrence[:, :, None] == slot_range[None, None, :]
    ).astype(jnp.int32)
    slot_valid = jnp.sum(slot_match, axis=0)
    slot_token = jnp.sum(slot_match * position_range[:, None, None], axis=0)
    slot_rank = jnp.sum(slot_match * rank_by_token[:, :, None], axis=0)
    send_rank = jnp.where((slot_valid > 0) & (slot_rank < capacity), slot_rank, -1)
    half_index = jnp.arange(members, dtype=jnp.int32) % 2
    token_layout = jnp.transpose(group_layout(slot_token, groups, members, expert_most), (1, 0, 2))
    rank_layout = jnp.transpose(group_layout(send_rank, groups, members, expert_most), (1, 0, 2))
    feature_rows = activations.reshape(tok_count * 2, half_width)
    send_rows = jnp.take(feature_rows, token_layout * 2 + half_index[:, None, None], axis=0)
    got_rows, got_rank = (
        lax.all_to_all(
            lax.all_to_all(send_rows, "group", split_axis=1, concat_axis=1, tiled=True),
            "ingroup",
            split_axis=0,
            concat_axis=0,
            tiled=True,
        ),
        lax.all_to_all(
            lax.all_to_all(rank_layout, "group", split_axis=1, concat_axis=1, tiled=True),
            "ingroup",
            split_axis=0,
            concat_axis=0,
            tiled=True,
        ),
    )
    slot_total = members * groups * expert_most
    flat_rank = got_rank.reshape(slot_total)
    flat_rows = got_rows.reshape(slot_total, half_width)
    target = jnp.where(flat_rank >= 0, flat_rank, capacity)
    source_of = (
        jnp.zeros((capacity,), jnp.int32)
        .at[target]
        .set(jnp.arange(slot_total, dtype=jnp.int32), mode="drop")
    )
    filled = jnp.zeros((capacity,), jnp.bool_).at[target].set(True, mode="drop")
    expert_rows = jnp.where(
        filled[:, None], jnp.take(flat_rows, source_of, axis=0), jnp.zeros((), activations.dtype)
    )
    gate_part = jnp.dot(expert_rows, gate_weights[0], preferred_element_type=jnp.float32).astype(
        jnp.bfloat16
    )
    up_part = jnp.dot(expert_rows, up_weights[0], preferred_element_type=jnp.float32).astype(
        jnp.bfloat16
    )
    other_gate, other_up = from_partner((gate_part, up_part), "ingroup", 0)
    gate_sum = gate_part.astype(jnp.float32) + other_gate.astype(jnp.float32)
    up_sum = up_part.astype(jnp.float32) + other_up.astype(jnp.float32)
    hidden = (jax.nn.silu(gate_sum) * up_sum).astype(jnp.bfloat16)
    expert_out = jnp.dot(hidden, down_weights[0], preferred_element_type=jnp.float32).astype(
        jnp.bfloat16
    )
    back_rows = jnp.take(expert_out, jnp.clip(flat_rank, 0, capacity - 1), axis=0)
    back_rows = jnp.where((flat_rank >= 0)[:, None], back_rows, jnp.zeros((), jnp.bfloat16))
    back_rows = back_rows.reshape(members, groups, expert_most, half_width)
    pick_group = expert_ids // per_group
    returned = lax.all_to_all(
        lax.all_to_all(back_rows, "group", split_axis=1, concat_axis=1, tiled=True),
        "ingroup",
        split_axis=0,
        concat_axis=0,
        tiled=True,
    )
    pick_member = expert_ids % per_group * 2
    halves = jnp.arange(2, dtype=jnp.int32)
    flat_pick = (
        (pick_member[:, :, None] + halves[None, None, :]) * groups + pick_group[:, :, None]
    ) * expert_most + pick_occurrence[:, :, None]
    gathered = jnp.take(returned.reshape(slot_total, half_width), flat_pick, axis=0)
    terms = routing[:, :, None] * gathered.reshape(tok_count, top_picks, model_width).astype(
        jnp.float32
    )
    pick_range = jnp.arange(top_picks, dtype=jnp.int32)
    not_self = (pick_range[:, None] != pick_range[None, :]).astype(jnp.int32)
    same_other = (pick_group[:, :, None] == pick_group[:, None, :]).astype(jnp.int32) * not_self[
        None, :, :
    ]
    partner = jnp.sum(same_other * pick_range[None, None, :], axis=2)
    partner_terms = jnp.take_along_axis(terms, partner[:, :, None], axis=1)
    paired = terms + partner_terms
    rounded = lax.optimization_barrier(paired.astype(jnp.bfloat16)).astype(jnp.float32)
    combined = 0.5 * jnp.sum(rounded, axis=1)
    return combined.astype(jnp.bfloat16)


def solution(mesh):
    return jax.shard_map(
        per_device,
        mesh=mesh,
        in_specs=(
            P(("group", "ingroup"), None),
            P(("group", "ingroup"), None, None),
            P(("group", "ingroup"), None, None),
            P(("group", "ingroup"), None, None),
            P(("group", "ingroup"), None),
            P(("group", "ingroup"), None),
            P(("group", "ingroup")),
        ),
        out_specs=P(("group", "ingroup"), None),
        check_vma=False,
    )
```

profile of v0, /device:TPU:1, one launch (start us, length us, event | category | flops | bytes accessed | tf_op | source)
XLA Modules:
  0.0 716.8 jit_solution(8007721992500397717)
XLA Ops:
  2.1 67.0 %all-gather.1 = s32[256,1,256]{2,1,0:T(1,128)S(1)} all-gather(s32[1,1,256]{2,1,0:T(1,128)S(1)} %bitcast.53), channel_id=2, replica_groups=mesh['group'=16,'ingroup'=16] {'group','ingroup'}, dimensions={0}, use_global_device_ids=true | all-gather | bytes 263168 | tf_op jit(solution)/shard_map/all_gather | solution.py:44
  85.5 9.6 %reshape.253 = bf16[16,16,6,1792]{3,2,1,0:T(8,128)(2,1)} reshape(bf16[1536,1792]{1,0:T(8,128)(2,1)} %gather_fusion) | data formatting | bytes 11010048 | tf_op jit(solution)/shard_map/jit(_take)/gather | solution.py:72
  112.2 80.3 %all-to-all-done.2 = bf16[16,16,6,1792]{3,0,2,1:T(8,128)(2,1)} async-done(((bf16[16,16,6,1792]{3,0,2,1:T(8,128)(2,1)}), bf16[16,16,6,1792]{3,0,2,1:T(8,128)(2,1)}, u32[]{:S(2)}, u32[]{:S(2)}) %all-to-all-start.2) | async-done | bytes 5505056 | tf_op jit(solution)/shard_map/all_to_all | solution.py:75
  198.8 7.9 %copy.151 = bf16[16,16,6,1792]{3,1,2,0:T(8,128)(2,1)} copy(bf16[16,16,6,1792]{3,0,2,1:T(8,128)(2,1)} %all-to-all-done.2) | data formatting | bytes 11010048 | tf_op jit(solution)/shard_map/all_to_all | solution.py:75
  206.7 7.2 %all-to-all-start.3 = ((bf16[16,16,6,1792]{3,1,2,0:T(8,128)(2,1)}), bf16[16,16,6,1792]{3,1,2,0:T(8,128)(2,1)}, u32[]{:S(2)}, u32[]{:S(2)}) async-start(bf16[16,16,6,1792]{3,1,2,0:T(8,128)(2,1)} %copy.151), calls=%async_computation.3 | async-start | bytes 11010048 | tf_op jit(solution)/shard_map/all_to_all | solution.py:74
  220.5 11.6 %scatter_custom_fusion = pred[1024]{0:T(1024)(128)(4,1)S(1)} fusion(s32[1536]{0:T(1024)S(1)} %get-tuple-element.13, pred[1536]{0:T(1024)(128)(4,1)S(1)} %broadcast.331, pred[]{:T(512)} %constant.148.clone.1), kind=kCustom, calls=%fused_computation.100 | custom fusion | bytes 1025 | tf_op jit(solution)/shard_map/scatter | solution.py:98
  232.2 103.5 %all-to-all-done.3 = bf16[16,16,6,1792]{3,1,2,0:T(8,128)(2,1)} async-done(((bf16[16,16,6,1792]{3,1,2,0:T(8,128)(2,1)}), bf16[16,16,6,1792]{3,1,2,0:T(8,128)(2,1)}, u32[]{:S(2)}, u32[]{:S(2)}) %all-to-all-start.3) | async-done | bytes 5505056 | tf_op jit(solution)/shard_map/all_to_all | solution.py:74
  335.7 7.7 %copy.152 = bf16[16,16,6,1792]{3,2,1,0:T(8,128)(2,1)} copy(bf16[16,16,6,1792]{3,1,2,0:T(8,128)(2,1)} %all-to-all-done.3) | data formatting | bytes 11010048 | tf_op jit(solution)/shard_map/all_to_all | solution.py:74
  343.3 9.7 %reshape.249 = bf16[1536,1792]{1,0:T(8,128)(2,1)} reshape(bf16[16,16,6,1792]{3,2,1,0:T(8,128)(2,1)} %copy.152) | data formatting | bytes 11010048 | tf_op jit(solution)/shard_map/reshape | solution.py:91
  353.0 11.2 %gather_fusion.1 = bf16[1024,1792]{1,0:T(8,128)(2,1)} fusion(bf16[1536,1792]{1,0:T(8,128)(2,1)} %reshape.249, s32[1024]{0:T(1024)S(1)} %fusion.37), kind=kCustom, calls=%fused_computation.1 | custom fusion | bytes 7344128 | tf_op jit(solution)/shard_map/jit(_take)/gather | solution.py:100
  364.2 7.3 %fusion.10 = bf16[1024,1024]{1,0:T(8,128)(2,1)S(1)} fusion(bf16[1,1792,1024]{2,1,0:T(8,128)(2,1)} %param.8, bf16[1024,1792]{1,0:T(8,128)(2,1)} %gather_fusion.1, pred[1024]{0:T(1024)(128)(4,1)S(1)} %compare_and_fusion.3, pred[1024]{0:T(1024)(128)(4,1)S(1)} %scatter_custom_fusion), kind=kOutput, calls=%fused_computation.28 | convolution fusion | flops 3762814976 | bytes 9439232 | tf_op jit(solution)/shard_map/dot_general | solution.py:102
  382.7 10.9 %convolution_convert_fusion = bf16[1024,1792]{1,0:T(8,128)(2,1)} fusion(bf16[1,1024,1792]{2,1,0:T(8,128)(2,1)} %param.10, bf16[1024,1024]{1,0:T(8,128)(2,1)} %collective-permute-done.1, bf16[1024,1024]{1,0:T(8,128)(2,1)} %fusion.13, bf16[1024,1024]{1,0:T(8,128)(2,1)} %collective-permute-done, bf16[1024,1024]{1,0:T(8,128)(2,1)S(1)} %fusion.10), kind=kOutput, calls=%fused_computation.18 | convolution fusion | flops 3772514304 | bytes 15728640 | tf_op jit(solution)/shard_map/dot_general | solution.py:112
  393.6 13.9 %gather_fusion.2 = bf16[1536,1792]{1,0:T(8,128)(2,1)} fusion(bf16[1024,1792]{1,0:T(8,128)(2,1)} %convolution_convert_fusion, s32[2048]{0:T(1024)S(1)} %pad_clamp_fusion), kind=kCustom, calls=%fused_computation.2 | custom fusion | bytes 11016192 | tf_op jit(solution)/shard_map/jit(_take)/gather | solution.py:115
  407.5 9.6 %gather.25 = bf16[16,16,6,1792]{3,2,1,0:T(8,128)(2,1)} reshape(bf16[1536,1792]{1,0:T(8,128)(2,1)} %gather_fusion.2) | data formatting | bytes 11010048 | tf_op jit(solution)/shard_map/jit(_take)/gather | solution.py:115
  424.5 69.9 %all_to_all.30 = bf16[16,16,6,1792]{3,0,2,1:T(8,128)(2,1)S(1)} all-to-all(bf16[16,16,6,1792]{3,0,2,1:T(8,128)(2,1)S(1)} %copy.153), channel_id=1, replica_groups=mesh['group'=16,'ingroup'=16] {'group'}, dimensions={1} | all-to-all | bytes 11010048 | tf_op jit(solution)/shard_map/all_to_all | solution.py:120
  510.2 117.6 %all-to-all-done.5 = bf16[16,16,6,1792]{3,1,2,0:T(8,128)(2,1)} async-done(((bf16[16,16,6,1792]{3,1,2,0:T(8,128)(2,1)}), bf16[16,16,6,1792]{3,1,2,0:T(8,128)(2,1)}, u32[]{:S(2)}, u32[]{:S(2)}) %all-to-all-start.5) | async-done | bytes 5505056 | tf_op jit(solution)/shard_map/all_to_all | solution.py:119
  627.7 7.7 %copy.155 = bf16[16,16,6,1792]{3,2,1,0:T(8,128)(2,1)} copy(bf16[16,16,6,1792]{3,1,2,0:T(8,128)(2,1)} %all-to-all-done.5) | data formatting | bytes 11010048 | tf_op jit(solution)/shard_map/all_to_all | solution.py:119
  635.4 9.7 %reshape.250 = bf16[1536,1792]{1,0:T(8,128)(2,1)} reshape(bf16[16,16,6,1792]{3,2,1,0:T(8,128)(2,1)} %copy.155) | data formatting | bytes 11010048 | tf_op jit(solution)/shard_map/reshape | solution.py:131
  645.1 11.2 %gather_fusion.3 = bf16[1024,1792]{1,0:T(8,128)(2,1)} fusion(bf16[1536,1792]{1,0:T(8,128)(2,1)} %reshape.250, s32[1024]{0:T(1024)S(1)} %broadcast_clamp_fusion), kind=kCustom, calls=%fused_computation.3 | custom fusion | bytes 7344128 | tf_op jit(solution)/shard_map/jit(_take)/gather | solution.py:131
  656.3 8.6 %reshape.277 = bf16[64,8,2,1792]{3,2,1,0:T(2,128)(2,1)} reshape(bf16[1024,1792]{1,0:T(8,128)(2,1)} %gather_fusion.3) | data formatting | bytes 7340032 | tf_op jit(solution)/shard_map/jit(_take)/gather | solution.py:131
  664.9 8.5 %fusion.3 = f32[64,8,2,1792]{3,2,1,0:T(2,128)} fusion(bf16[64,8,2,1792]{3,2,1,0:T(2,128)(2,1)} %reshape.277, pred[64,8,2]{2,1,0:T(8,128)(4,1)S(1)} %copy.140), kind=kLoop, calls=%fused_computation.19 | loop fusion | flops 3670016 | bytes 11011072 | tf_op jit(solution)/shard_map/convert_element_type | solution.py:132
  673.4 10.0 %reshape.251 = f32[64,8,3584]{2,1,0:T(8,128)} reshape(f32[64,8,2,1792]{3,2,1,0:T(2,128)} %fusion.3) | data formatting | bytes 14680064 | tf_op jit(solution)/shard_map/convert_element_type | solution.py:132
  683.4 6.9 broadcast_multiply_fusion
  690.3 16.6 %gather_fusion.4 = f32[512,3584]{1,0:T(8,128)} fusion(f32[64,8,3584]{2,1,0:T(8,128)} %broadcast_multiply_fusion, s32[512]{0:T(512)S(1)} %reshape.284), kind=kCustom, calls=%fused_computation.4 | custom fusion | bytes 14684160 | tf_op jit(solution)/shard_map/jit(take_along_axis)/gather | solution.py:141
  (103 shorter events, 92.0 us)
Async XLA Ops:
  0.0 78.6 %copy-start.1 = (bf16[64,3584]{1,0:T(8,128)(2,1)S(1)}, bf16[64,3584]{1,0:T(8,128)(2,1)}, u32[]{:S(2)}) copy-start(bf16[64,3584]{1,0:T(8,128)(2,1)} %param.7) | copy-start | bytes 1376260
  73.7 31.1 %all-to-all-start = ((s32[16,16,6]{0,2,1:T(8,128)}), s32[16,16,6]{0,2,1:T(8,128)S(1)}, u32[]{:S(2)}, u32[]{:S(2)}) async-start(s32[16,16,6]{0,2,1:T(8,128)} %copy.142), calls=%async_computation | async-start | bytes 131072 | tf_op jit(solution)/shard_map/all_to_all | solution.py:82
  104.8 87.7 %all-to-all-start.2 = ((bf16[16,16,6,1792]{3,0,2,1:T(8,128)(2,1)}), bf16[16,16,6,1792]{3,0,2,1:T(8,128)(2,1)}, u32[]{:S(2)}, u32[]{:S(2)}) async-start(bf16[16,16,6,1792]{3,0,2,1:T(8,128)(2,1)} %copy.150), calls=%async_computation.2 | async-start | bytes 11010048 | tf_op jit(solution)/shard_map/all_to_all | solution.py:75
  192.5 14.2 %all-to-all-start.1 = ((s32[16,16,6]{1,2,0:T(8,128)}), s32[16,16,6]{1,2,0:T(8,128)S(1)}, u32[]{:S(2)}, u32[]{:S(2)}) async-start(s32[16,16,6]{1,2,0:T(8,128)} %copy.143), calls=%async_computation.1 | async-start | bytes 131072 | tf_op jit(solution)/shard_map/all_to_all | solution.py:81
  206.7 129.0 %all-to-all-start.3 = ((bf16[16,16,6,1792]{3,1,2,0:T(8,128)(2,1)}), bf16[16,16,6,1792]{3,1,2,0:T(8,128)(2,1)}, u32[]{:S(2)}, u32[]{:S(2)}) async-start(bf16[16,16,6,1792]{3,1,2,0:T(8,128)(2,1)} %copy.151), calls=%async_computation.3 | async-start | bytes 11010048 | tf_op jit(solution)/shard_map/all_to_all | solution.py:74
  364.2 8.3 %copy-start = (bf16[1024,1792]{1,0:T(8,128)(2,1)S(1)}, bf16[1024,1792]{1,0:T(8,128)(2,1)}, u32[]{:S(2)}) copy-start(bf16[1024,1792]{1,0:T(8,128)(2,1)} %gather_fusion.1) | copy-start | bytes 11010052
  364.2 8.3 %copy-start.3 = (bf16[1,1792,1024]{2,1,0:T(8,128)(2,1)S(1)}, bf16[1,1792,1024]{2,1,0:T(8,128)(2,1)}, u32[]{:S(2)}) copy-start(bf16[1,1792,1024]{2,1,0:T(8,128)(2,1)} %param.9) | copy-start | bytes 11010052
  371.5 7.2 %collective-permute-start = (bf16[1024,1024]{1,0:T(8,128)(2,1)S(1)}, bf16[1024,1024]{1,0:T(8,128)(2,1)}, u32[]{:S(2)}, u32[]{:S(2)}) collective-permute-start(bf16[1024,1024]{1,0:T(8,128)(2,1)S(1)} %fusion.10), channel_id=1, source_target_pairs={{0,1},{1,0},{2,3},{3,2},{4,5},{5,4},{6,7},{7,6},{8,9},{9,8},{10,11... | collective-permute-start | bytes 6291464 | tf_op jit(solution)/shard_map/ppermute | solution.py:10
  378.1 4.7 collective-permute-start.1
  499.8 9.5 %copy-start.2 = (s32[64,8]{0,1:T(8,128)S(1)}, s32[64,8]{0,1:T(8,128)}, u32[]{:S(2)}) copy-start(s32[64,8]{0,1:T(8,128)} %param.12) | copy-start | bytes 6148
  499.8 128.0 %all-to-all-start.5 = ((bf16[16,16,6,1792]{3,1,2,0:T(8,128)(2,1)}), bf16[16,16,6,1792]{3,1,2,0:T(8,128)(2,1)}, u32[]{:S(2)}, u32[]{:S(2)}) async-start(bf16[16,16,6,1792]{3,1,2,0:T(8,128)(2,1)} %copy.154), calls=%async_computation.5 | async-start | bytes 11010048 | tf_op jit(solution)/shard_map/all_to_all | solution.py:119
where the time goes:
time: 726 us; the launch traced here: 717 us
  waiting for transfers between devices  305 us (42%)
  local copies, waits for them, and re-layouts  177 us (24%)
  blocking collectives  137 us (19%)
  other arithmetic  38.8 us (5%)
  starting transfers between devices  31.8 us (4%)
  matrix products  25.6 us (4%)
    all_to_all x1, waiting for transfers between devices, per_device(): lax.all_to_all(lax.all_to_all(back_rows, 'group', split_axis=1, concat_ax...  118 us
    all_to_all x1, waiting for transfers between devices, per_device(): lax.all_to_all(lax.all_to_all(send_rows, 'group', split_axis=1, concat_ax...  104 us
    all_to_all x1, waiting for transfers between devices, per_device(): lax.all_to_all(send_rows, 'group', split_axis=1, concat_axis=1, tiled=True)  80.3 us
    all_to_all x1, blocking collectives, per_device(): lax.all_to_all(back_rows, 'group', split_axis=1, concat_axis=1, tiled=True)  69.9 us
    all_gather x1, blocking collectives, per_device(): piece = lax.all_gather(packed, ('group', 'ingroup'), axis=0, tiled=True)  67 us
    gather x2, local copies, waits for them, and re-layouts, per_device(): jnp.take(expert_out, jnp.clip(flat_rank, 0, capacity - 1), axis=0)  23.4 us
    gather x2, local copies, waits for them, and re-layouts, per_device(): jnp.take(returned.reshape(slot_total, half_width), flat_pick, axis=0)  19.8 us
    gather x3, local copies, waits for them, and re-layouts, per_device(): partner_terms = jnp.take_along_axis(terms, partner[:, :, None], axis=1)  16.8 us
  transfers between devices with their start and end apart: 7, of which 4 were waited for; matrix products, arithmetic and copies ran while one was open for 9% of the time, Pallas kernels for 0%

commit v1 on v0

--- a/solution.py
+++ b/solution.py
@@ -41,7 +41,12 @@
     flat_bits = own_counts.reshape(-1, 32)
     packed = jnp.sum(jnp.left_shift(flat_bits, shifts[None, :]), axis=1)[None, :]
     my_index = lax.axis_index(("group", "ingroup"))
-    piece = lax.all_gather(packed, ("group", "ingroup"), axis=0, tiled=True)
+    piece = jnp.concatenate(
+        lax.all_to_all(
+            jnp.stack([packed] * lax.axis_size(("group", "ingroup"))), ("group", "ingroup"), 0, 0
+        ),
+        axis=0,
+    )
     bit_table = jnp.bitwise_and(jnp.right_shift(piece[:, :, None], shifts[None, None, :]), 1)
     bit_table = bit_table.reshape(piece.shape[0], experts, tok_count)
     source_index = jnp.arange(piece.shape[0], dtype=jnp.int32)

time: 726 us -> 689 us (0.949)
  blocking collectives: 137 us -> 69.8 us
  waiting for transfers between devices: 305 us -> 320 us
  starting transfers between devices: 31.8 us -> 46 us
    all_gather x1 -> x0, blocking collectives: 67 us -> none  [per_device(): piece = lax.all_gather(packed, ('group', 'ingroup'), axis=0, tiled=True)]
    all_to_all x0 -> x1, starting transfers between devices: none -> 15.7 us  [per_device(): lax.all_to_all(jnp.stack([packed] * lax.axis_size(('group', 'ingroup'))),...]
    all_to_all x0 -> x1, waiting for transfers between devices: none -> 14.6 us  [per_device(): lax.all_to_all(jnp.stack([packed] * lax.axis_size(('group', 'ingroup'))),...]
  transfers between devices with their start and end apart: 7 -> 8, of which waited for: 4 -> 5; matrix products, arithmetic and copies ran while one was open for 9% -> 7% of each run, Pallas kernels for 0% -> 0%
where the time goes in v1:
time: 689 us; the launch traced here: 679 us
  waiting for transfers between devices  320 us (46%)
  local copies, waits for them, and re-layouts  179 us (26%)
  blocking collectives  69.8 us (10%)
  starting transfers between devices  46 us (7%)
  other arithmetic  38.8 us (6%)
  matrix products  24.9 us (4%)
    all_to_all x1, waiting for transfers between devices, per_device(): lax.all_to_all(lax.all_to_all(back_rows, 'group', split_axis=1, concat_ax...  118 us
    all_to_all x1, waiting for transfers between devices, per_device(): lax.all_to_all(lax.all_to_all(send_rows, 'group', split_axis=1, concat_ax...  104 us
    all_to_all x1, waiting for transfers between devices, per_device(): lax.all_to_all(send_rows, 'group', split_axis=1, concat_axis=1, tiled=True)  80.2 us
    all_to_all x1, blocking collectives, per_device(): lax.all_to_all(back_rows, 'group', split_axis=1, concat_axis=1, tiled=True)  69.8 us
    gather x2, local copies, waits for them, and re-layouts, per_device(): jnp.take(expert_out, jnp.clip(flat_rank, 0, capacity - 1), axis=0)  23.4 us
    gather x2, local copies, waits for them, and re-layouts, per_device(): jnp.take(returned.reshape(slot_total, half_width), flat_pick, axis=0)  19.8 us
    gather x3, local copies, waits for them, and re-layouts, per_device(): partner_terms = jnp.take_along_axis(terms, partner[:, :, None], axis=1)  16.8 us
    gather x2, local copies, waits for them, and re-layouts, per_device(): jnp.take(feature_rows, token_layout * 2 + half_index[:, None, None], axis=0)  16.3 us
  transfers between devices with their start and end apart: 8, of which 5 were waited for; matrix products, arithmetic and copies ran while one was open for 7% of the time, Pallas kernels for 0%

profile of v1, /device:TPU:1, one launch (start us, length us, event | category | flops | bytes accessed | tf_op | source)
XLA Modules:
  0.0 679.5 jit_solution(15337387334209456265)
XLA Ops:
  2.9 15.7 %all-to-all-start = ((s32[256,1,256]{2,1,0:T(1,128)}), s32[256,1,256]{2,1,0:T(1,128)S(1)}, u32[]{:S(2)}, u32[]{:S(2)}) async-start(s32[256,1,256]{2,1,0:T(1,128)} %stack.3), calls=%async_computation | async-start | bytes 524288 | tf_op jit(solution)/shard_map/all_to_all | solution.py:45
  19.9 14.6 %all-to-all-done = s32[256,1,256]{2,1,0:T(1,128)S(1)} async-done(((s32[256,1,256]{2,1,0:T(1,128)}), s32[256,1,256]{2,1,0:T(1,128)S(1)}, u32[]{:S(2)}, u32[]{:S(2)}) %all-to-all-start) | async-done | bytes 262176 | tf_op jit(solution)/shard_map/all_to_all | solution.py:45
  44.6 9.6 %reshape.255 = bf16[16,16,6,1792]{3,2,1,0:T(8,128)(2,1)} reshape(bf16[1536,1792]{1,0:T(8,128)(2,1)} %gather_fusion) | data formatting | bytes 11010048 | tf_op jit(solution)/shard_map/jit(_take)/gather | solution.py:77
  75.8 80.2 %all-to-all-done.3 = bf16[16,16,6,1792]{3,0,2,1:T(8,128)(2,1)} async-done(((bf16[16,16,6,1792]{3,0,2,1:T(8,128)(2,1)}), bf16[16,16,6,1792]{3,0,2,1:T(8,128)(2,1)}, u32[]{:S(2)}, u32[]{:S(2)}) %all-to-all-start.3) | async-done | bytes 5505056 | tf_op jit(solution)/shard_map/all_to_all | solution.py:80
  161.6 7.9 %copy.186 = bf16[16,16,6,1792]{3,1,2,0:T(8,128)(2,1)} copy(bf16[16,16,6,1792]{3,0,2,1:T(8,128)(2,1)} %all-to-all-done.3) | data formatting | bytes 11010048 | tf_op jit(solution)/shard_map/all_to_all | solution.py:80
  169.5 7.3 %all-to-all-start.4 = ((bf16[16,16,6,1792]{3,1,2,0:T(8,128)(2,1)}), bf16[16,16,6,1792]{3,1,2,0:T(8,128)(2,1)}, u32[]{:S(2)}, u32[]{:S(2)}) async-start(bf16[16,16,6,1792]{3,1,2,0:T(8,128)(2,1)} %copy.186), calls=%async_computation.4 | async-start | bytes 11010048 | tf_op jit(solution)/shard_map/all_to_all | solution.py:79
  183.3 11.6 %scatter_custom_fusion = pred[1024]{0:T(1024)(128)(4,1)S(1)} fusion(s32[1536]{0:T(1024)S(1)} %get-tuple-element.13, pred[1536]{0:T(1024)(128)(4,1)S(1)} %broadcast.332, pred[]{:T(512)} %constant.148.clone.1), kind=kCustom, calls=%fused_computation.100 | custom fusion | bytes 1025 | tf_op jit(solution)/shard_map/scatter | solution.py:103
  195.0 103.5 %all-to-all-done.4 = bf16[16,16,6,1792]{3,1,2,0:T(8,128)(2,1)} async-done(((bf16[16,16,6,1792]{3,1,2,0:T(8,128)(2,1)}), bf16[16,16,6,1792]{3,1,2,0:T(8,128)(2,1)}, u32[]{:S(2)}, u32[]{:S(2)}) %all-to-all-start.4) | async-done | bytes 5505056 | tf_op jit(solution)/shard_map/all_to_all | solution.py:79
  298.5 7.7 %copy.187 = bf16[16,16,6,1792]{3,2,1,0:T(8,128)(2,1)} copy(bf16[16,16,6,1792]{3,1,2,0:T(8,128)(2,1)} %all-to-all-done.4) | data formatting | bytes 11010048 | tf_op jit(solution)/shard_map/all_to_all | solution.py:79
  306.2 9.7 %reshape.251 = bf16[1536,1792]{1,0:T(8,128)(2,1)} reshape(bf16[16,16,6,1792]{3,2,1,0:T(8,128)(2,1)} %copy.187) | data formatting | bytes 11010048 | tf_op jit(solution)/shard_map/reshape | solution.py:96
  315.8 11.2 %gather_fusion.1 = bf16[1024,1792]{1,0:T(8,128)(2,1)} fusion(bf16[1536,1792]{1,0:T(8,128)(2,1)} %reshape.251, s32[1024]{0:T(1024)S(1)} %fusion.37), kind=kCustom, calls=%fused_computation.1 | custom fusion | bytes 7344128 | tf_op jit(solution)/shard_map/jit(_take)/gather | solution.py:105
  327.0 7.3 %fusion.10 = bf16[1024,1024]{1,0:T(8,128)(2,1)S(1)} fusion(bf16[1,1792,1024]{2,1,0:T(8,128)(2,1)} %param.8, bf16[1024,1792]{1,0:T(8,128)(2,1)} %gather_fusion.1, pred[1024]{0:T(1024)(128)(4,1)S(1)} %compare_and_fusion.3, pred[1024]{0:T(1024)(128)(4,1)S(1)} %scatter_custom_fusion), kind=kOutput, calls=%fused_computation.28 | convolution fusion | flops 3762814976 | bytes 9439232 | tf_op jit(solution)/shard_map/dot_general | solution.py:107
  345.5 10.8 %convolution_convert_fusion = bf16[1024,1792]{1,0:T(8,128)(2,1)} fusion(bf16[1,1024,1792]{2,1,0:T(8,128)(2,1)} %param.10, bf16[1024,1024]{1,0:T(8,128)(2,1)} %collective-permute-done.1, bf16[1024,1024]{1,0:T(8,128)(2,1)} %fusion.13, bf16[1024,1024]{1,0:T(8,128)(2,1)} %collective-permute-done, bf16[1024,1024]{1,0:T(8,128)(2,1)S(1)} %fusion.10), kind=kOutput, calls=%fused_computation.18 | convolution fusion | flops 3772514304 | bytes 15728640 | tf_op jit(solution)/shard_map/dot_general | solution.py:117
  356.4 13.9 %gather_fusion.2 = bf16[1536,1792]{1,0:T(8,128)(2,1)} fusion(bf16[1024,1792]{1,0:T(8,128)(2,1)} %convolution_convert_fusion, s32[2048]{0:T(1024)S(1)} %pad_clamp_fusion), kind=kCustom, calls=%fused_computation.2 | custom fusion | bytes 11016192 | tf_op jit(solution)/shard_map/jit(_take)/gather | solution.py:120
  370.2 9.6 %gather.25 = bf16[16,16,6,1792]{3,2,1,0:T(8,128)(2,1)} reshape(bf16[1536,1792]{1,0:T(8,128)(2,1)} %gather_fusion.2) | data formatting | bytes 11010048 | tf_op jit(solution)/shard_map/jit(_take)/gather | solution.py:120
  387.2 69.8 %all_to_all.35 = bf16[16,16,6,1792]{3,0,2,1:T(8,128)(2,1)S(1)} all-to-all(bf16[16,16,6,1792]{3,0,2,1:T(8,128)(2,1)S(1)} %copy.188), channel_id=1, replica_groups=mesh['group'=16,'ingroup'=16] {'group'}, dimensions={1} | all-to-all | bytes 11010048 | tf_op jit(solution)/shard_map/all_to_all | solution.py:125
  472.9 117.6 %all-to-all-done.6 = bf16[16,16,6,1792]{3,1,2,0:T(8,128)(2,1)} async-done(((bf16[16,16,6,1792]{3,1,2,0:T(8,128)(2,1)}), bf16[16,16,6,1792]{3,1,2,0:T(8,128)(2,1)}, u32[]{:S(2)}, u32[]{:S(2)}) %all-to-all-start.6) | async-done | bytes 5505056 | tf_op jit(solution)/shard_map/all_to_all | solution.py:124
  590.4 7.7 %copy.190 = bf16[16,16,6,1792]{3,2,1,0:T(8,128)(2,1)} copy(bf16[16,16,6,1792]{3,1,2,0:T(8,128)(2,1)} %all-to-all-done.6) | data formatting | bytes 11010048 | tf_op jit(solution)/shard_map/all_to_all | solution.py:124
  598.1 9.7 %reshape.252 = bf16[1536,1792]{1,0:T(8,128)(2,1)} reshape(bf16[16,16,6,1792]{3,2,1,0:T(8,128)(2,1)} %copy.190) | data formatting | bytes 11010048 | tf_op jit(solution)/shard_map/reshape | solution.py:136
  607.8 11.2 %gather_fusion.3 = bf16[1024,1792]{1,0:T(8,128)(2,1)} fusion(bf16[1536,1792]{1,0:T(8,128)(2,1)} %reshape.252, s32[1024]{0:T(1024)S(1)} %broadcast_clamp_fusion), kind=kCustom, calls=%fused_computation.3 | custom fusion | bytes 7344128 | tf_op jit(solution)/shard_map/jit(_take)/gather | solution.py:136
  619.0 8.6 %reshape.279 = bf16[64,8,2,1792]{3,2,1,0:T(2,128)(2,1)} reshape(bf16[1024,1792]{1,0:T(8,128)(2,1)} %gather_fusion.3) | data formatting | bytes 7340032 | tf_op jit(solution)/shard_map/jit(_take)/gather | solution.py:136
  627.6 8.5 %fusion.3 = f32[64,8,2,1792]{3,2,1,0:T(2,128)} fusion(bf16[64,8,2,1792]{3,2,1,0:T(2,128)(2,1)} %reshape.279, pred[64,8,2]{2,1,0:T(8,128)(4,1)S(1)} %copy.175), kind=kLoop, calls=%fused_computation.19 | loop fusion | flops 3670016 | bytes 11011072 | tf_op jit(solution)/shard_map/convert_element_type | solution.py:137
  636.1 10.0 %reshape.253 = f32[64,8,3584]{2,1,0:T(8,128)} reshape(f32[64,8,2,1792]{3,2,1,0:T(2,128)} %fusion.3) | data formatting | bytes 14680064 | tf_op jit(solution)/shard_map/convert_element_type | solution.py:137
  653.0 16.6 %gather_fusion.4 = f32[512,3584]{1,0:T(8,128)} fusion(f32[64,8,3584]{2,1,0:T(8,128)} %broadcast_multiply_fusion, s32[512]{0:T(512)S(1)} %reshape.286), kind=kCustom, calls=%fused_computation.4 | custom fusion | bytes 14684160 | tf_op jit(solution)/shard_map/jit(take_along_axis)/gather | solution.py:146
  (105 shorter events, 98.5 us)
Async XLA Ops:
  0.0 36.9 %copy-start.2 = (s32[64]{0:T(128)S(1)}, s32[64]{0:T(128)}, u32[]{:S(2)}) copy-start(s32[64]{0:T(128)} %param.13) | copy-start | bytes 772
  2.9 31.6 %all-to-all-start = ((s32[256,1,256]{2,1,0:T(1,128)}), s32[256,1,256]{2,1,0:T(1,128)S(1)}, u32[]{:S(2)}, u32[]{:S(2)}) async-start(s32[256,1,256]{2,1,0:T(1,128)} %stack.3), calls=%async_computation | async-start | bytes 524288 | tf_op jit(solution)/shard_map/all_to_all | solution.py:45
  55.5 13.0 %all-to-all-start.1 = ((s32[16,16,6]{0,2,1:T(8,128)}), s32[16,16,6]{0,2,1:T(8,128)S(1)}, u32[]{:S(2)}, u32[]{:S(2)}) async-start(s32[16,16,6]{0,2,1:T(8,128)} %copy.177), calls=%async_computation.1 | async-start | bytes 131072 | tf_op jit(solution)/shard_map/all_to_all | solution.py:87
  68.5 87.6 %all-to-all-start.3 = ((bf16[16,16,6,1792]{3,0,2,1:T(8,128)(2,1)}), bf16[16,16,6,1792]{3,0,2,1:T(8,128)(2,1)}, u32[]{:S(2)}, u32[]{:S(2)}) async-start(bf16[16,16,6,1792]{3,0,2,1:T(8,128)(2,1)} %copy.185), calls=%async_computation.3 | async-start | bytes 11010048 | tf_op jit(solution)/shard_map/all_to_all | solution.py:80
  156.0 13.5 %all-to-all-start.2 = ((s32[16,16,6]{1,2,0:T(8,128)}), s32[16,16,6]{1,2,0:T(8,128)S(1)}, u32[]{:S(2)}, u32[]{:S(2)}) async-start(s32[16,16,6]{1,2,0:T(8,128)} %copy.178), calls=%async_computation.2 | async-start | bytes 131072 | tf_op jit(solution)/shard_map/all_to_all | solution.py:86
  169.5 129.0 %all-to-all-start.4 = ((bf16[16,16,6,1792]{3,1,2,0:T(8,128)(2,1)}), bf16[16,16,6,1792]{3,1,2,0:T(8,128)(2,1)}, u32[]{:S(2)}, u32[]{:S(2)}) async-start(bf16[16,16,6,1792]{3,1,2,0:T(8,128)(2,1)} %copy.186), calls=%async_computation.4 | async-start | bytes 11010048 | tf_op jit(solution)/shard_map/all_to_all | solution.py:79
  327.0 8.3 %copy-start = (bf16[1024,1792]{1,0:T(8,128)(2,1)S(1)}, bf16[1024,1792]{1,0:T(8,128)(2,1)}, u32[]{:S(2)}) copy-start(bf16[1024,1792]{1,0:T(8,128)(2,1)} %gather_fusion.1) | copy-start | bytes 11010052
  327.0 8.3 %copy-start.3 = (bf16[1,1792,1024]{2,1,0:T(8,128)(2,1)S(1)}, bf16[1,1792,1024]{2,1,0:T(8,128)(2,1)}, u32[]{:S(2)}) copy-start(bf16[1,1792,1024]{2,1,0:T(8,128)(2,1)} %param.9) | copy-start | bytes 11010052
  334.3 7.2 %collective-permute-start = (bf16[1024,1024]{1,0:T(8,128)(2,1)S(1)}, bf16[1024,1024]{1,0:T(8,128)(2,1)}, u32[]{:S(2)}, u32[]{:S(2)}) collective-permute-start(bf16[1024,1024]{1,0:T(8,128)(2,1)S(1)} %fusion.10), channel_id=1, source_target_pairs={{0,1},{1,0},{2,3},{3,2},{4,5},{5,4},{6,7},{7,6},{8,9},{9,8},{10,11... | collective-permute-start | bytes 6291464 | tf_op jit(solution)/shard_map/ppermute | solution.py:10
  340.9 4.7 collective-permute-start.1
  462.5 6.4 copy-start.1
  462.5 128.0 %all-to-all-start.6 = ((bf16[16,16,6,1792]{3,1,2,0:T(8,128)(2,1)}), bf16[16,16,6,1792]{3,1,2,0:T(8,128)(2,1)}, u32[]{:S(2)}, u32[]{:S(2)}) async-start(bf16[16,16,6,1792]{3,1,2,0:T(8,128)(2,1)} %copy.189), calls=%async_computation.6 | async-start | bytes 11010048 | tf_op jit(solution)/shard_map/all_to_all | solution.py:124
